TPU v7x, 32 devices: a whole 2x2x4 slice. The times are simulated.
32 devices in a mesh: row: 4 (over y, core), col: 4 (over z), aux: 2 (over x).
Axes of the slice: x: 2, y: 2, z: 4, core: 2. Of those that a mesh axis runs over, the one named last changes fastest.
Arguments:
- integrals: bfloat16 [2, 128, 64, 3072], P('aux', ('row', 'col')), may hold values from -0.75 to 0.75
- block_mask: int32 [2, 64, 64], P('aux', ('row', 'col')), may hold values from 0 to 1, as said below
- block_slots: int32 [2, 64, 64], P('aux', ('row', 'col')), may hold values from -1 to 7, as said below
- orbitals: bfloat16 [64, 4096], replicated, may hold values from -0.21582031 to 0.21582031
Outputs:
- exchange_matrix: float32 [4096, 4, 1024], P(('row', 'aux'), None, 'col')
Inputs may be any that keep to these rules, and one draw needn't show every extreme that they name: `block_mask`: within one device's tile (one auxiliary batch, the mu blocks of one row and col index pair, all lambda blocks) between 1 and 8 blocks survive, and in some tile exactly 8. `block_slots`: the surviving blocks of a tile are numbered 0, 1, 2, ... in row-major order of (mu block, lambda block); blocks that did not survive hold -1, and packed slots past a tile's count hold data that is never read.
All inputs are finite; a program needn't handle non-finite values.
Results may differ from a plain program's by a relative error of at most 0.0017.
Values may be sent and summed in bfloat16 or wider, within the bound.
A program may use at most 128 MiB of HBM per device.

v0:
```python
import jax
import jax.numpy as jnp
from jax import lax
from jax.sharding import PartitionSpec as P


def half_transform(mask_tile, slot_tile, packed_tile, orbitals):
    capacity = packed_tile.shape[0]
    block_size = packed_tile.shape[1]
    row_blocks, block_count = mask_tile.shape
    occ_count = orbitals.shape[0]
    aux_count = packed_tile.shape[2] // block_size
    mask_flat = mask_tile.reshape(-1)
    slot_flat = slot_tile.reshape(-1)
    positions = jnp.arange(mask_flat.shape[0], dtype=jnp.int32)
    slot_ids = jnp.arange(capacity, dtype=jnp.int32)
    select = ((mask_flat[None, :] == 1) & (slot_flat[None, :] == slot_ids[:, None])).astype(
        jnp.int32
    )
    block_row = jnp.sum(select * (positions // block_count)[None, :], axis=1)
    lam_block = jnp.sum(select * (positions % block_count)[None, :], axis=1)
    present = jnp.sum(select, axis=1).astype(jnp.float32)
    weights = (block_row[:, None] == jnp.arange(row_blocks, dtype=jnp.int32)[None, :]).astype(
        jnp.float32
    ) * present[:, None]
    orbital_blocks = jnp.take(
        orbitals.reshape(occ_count, block_count, block_size), lam_block, axis=1
    )
    products = jnp.einsum(
        "isx,sxy->siy", orbital_blocks, packed_tile, preferred_element_type=jnp.float32
    )
    products = products.reshape(capacity, occ_count, aux_count, block_size)
    half_block = jnp.einsum("sb,siqm->iqbm", weights, products, precision=lax.Precision.HIGHEST)
    return half_block.reshape(occ_count, aux_count, row_blocks * block_size).astype(jnp.bfloat16)


def local(integrals, block_mask, block_slots, orbitals):
    half_local = half_transform(block_mask[0], block_slots[0], integrals[0], orbitals)
    occ_count, aux_count, local_rows = half_local.shape
    row_index = lax.axis_index("row")
    col_index = lax.axis_index("col")
    row_count = lax.axis_size("row")
    col_count = lax.axis_size("col")
    contract = (((0, 1), (0, 1)), ((), ()))
    gathered = lax.all_gather(half_local, ("row", "col"), axis=2, tiled=True)
    rows_panel = lax.dynamic_slice_in_dim(
        gathered, row_index * col_count * local_rows, col_count * local_rows, 2
    )
    grid_view = gathered.reshape(occ_count, aux_count, row_count, col_count, local_rows)
    column_panel = lax.dynamic_index_in_dim(grid_view, col_index, 3, keepdims=False)
    exchange_tile = lax.dot_general(
        rows_panel, column_panel, contract, preferred_element_type=jnp.float32
    )
    return lax.psum_scatter(exchange_tile, "aux", scatter_dimension=0, tiled=True)


def solution(mesh):
    placed = (
        P("aux", ("row", "col"), None, None),
        P("aux", ("row", "col"), None),
        P("aux", ("row", "col"), None),
        P(),
    )
    return jax.shard_map(
        local, mesh=mesh, in_specs=placed, out_specs=P(("row", "aux"), None, "col"), check_vma=False
    )
```

profile of v0, /device:TPU:7, one launch (start us, length us, event | category | flops | bytes accessed | tf_op | source)
XLA Modules:
  0.0 327.9 jit_solution(13120239253641608262)
XLA Ops:
  6.5 0.0 copy-start
  6.5 0.0 all-gather.2.cloned.1.call-start
  6.5 0.8 broadcast_compare_fusion
  7.4 0.1 eq.48
  7.5 0.8 eq.49
  8.3 0.1 select_reduce_fusion
  8.5 2.8 reshape.65
  11.2 2.9 copy.18
  14.1 1.8 gather_fusion
  15.9 0.0 copy-done
  15.9 3.6 %fusion.5 = f32[8,64,3072]{2,1,0:T(8,128)} fusion(bf16[1,8,64,3072]{3,2,1,0:T(8,128)(2,1)S(1)} %copy-done, bf16[8,64,64]{2,1,0:T(8,128)(2,1)S(1)} %gather_fusion, pred[8]{0:T(512)(128)(4,1)S(1)} %compare_and_fusion), kind=kOutput, calls=%fused_computation.7 | convolution fusion | flops 201359360 | bytes 9502728 | tf_op jit(solution)/shard_map/isx,sxy->siy/dot_general | solution.py:29
  19.6 10.0 %reshape.66 = f32[8,64,48,64]{3,2,1,0:T(8,128)} reshape(f32[8,64,3072]{2,1,0:T(8,128)} %fusion.5) | data formatting | bytes 12582912 | tf_op jit(solution)/shard_map/reshape | solution.py:32
  29.5 21.8 %convert_bitcast_fusion = bf16[64,48,4,64]{3,2,1,0:T(4,128)(2,1)S(1)} fusion(f32[8,64,48,64]{3,2,1,0:T(8,128)} %reshape.66, f32[8]{0:T(128)S(1)} %convert_element_type.21, s32[8]{0:T(128)S(1)} %get-tuple-element.5), kind=kOutput, calls=%fused_computation.9 | convolution fusion | flops 76283968 | bytes 7864384 | tf_op jit(solution)/shard_map/sb,siqm->iqbm/dot_general | solution.py:33
  51.3 3.0 convert_element_type.24
  54.3 3.2 copy.20
  57.5 0.0 all-gather.2.cloned.1.call-update
  57.5 0.0 reduce-scatter.2.cloned.1.call-start
  57.6 138.9 %all-gather.2.cloned.1.call-done = bf16[64,48,4096]{2,0,1:T(8,128)(2,1)} async-done(((bf16[64,48,256]{2,0,1:T(8,128)(2,1)}), bf16[64,48,4096]{2,0,1:T(8,128)(2,1)}) %all-gather.2.cloned.1.call-update) | async-done | bytes 25165840 | tf_op jit(solution)/shard_map/all_gather | solution.py:45
  196.5 41.3 %reshape.67 = bf16[64,48,4,4,256]{4,3,2,0,1:T(4,128)(2,1)} reshape(bf16[64,48,4096]{2,0,1:T(8,128)(2,1)} %all-gather.2.cloned.1.call-done) | data formatting | bytes 50331648 | tf_op jit(solution)/shard_map/reshape | solution.py:49
  237.8 14.7 %constant_dynamic-slice_fusion = bf16[64,48,4,1,256]{4,3,2,0,1:T(2,128)(2,1)S(1)} fusion(bf16[64,48,4,4,256]{4,3,2,0,1:T(4,128)(2,1)} %reshape.67, s32[]{:T(128)S(6)} %select_n.53), kind=kLoop, calls=%fused_computation.39 | loop fusion | bytes 12582916 | tf_op jit(solution)/shard_map/jit(dynamic_index_in_dim)/dynamic_slice | solution.py:50
  252.5 0.0 copy-start.1
  252.5 10.4 %fusion.9 = f32[1024,4,256]{2,0,1:T(8,128)} fusion(bf16[64,48,4,1,256]{4,3,2,0,1:T(2,128)(2,1)S(1)} %constant_dynamic-slice_fusion, bf16[64,48,4096]{2,0,1:T(8,128)(2,1)} %all-gather.2.cloned.1.call-done, s32[]{:T(128)S(6)} %select_n.52), kind=kOutput, calls=%fused_computation.10 | convolution fusion | flops 6442450944 | bytes 16777220 | tf_op jit(solution)/shard_map/dot_general | solution.py:51
  262.9 0.0 reduce-scatter.2.cloned.1.call-update
  262.9 53.9 %reduce-scatter.2.cloned.1.call-done = f32[512,4,256]{2,0,1:T(8,128)} async-done(((f32[1024,4,256]{2,0,1:T(8,128)}), f32[512,4,256]{2,0,1:T(8,128)}) %reduce-scatter.2.cloned.1.call-update) | async-done | bytes 2097168 | tf_op jit(solution)/shard_map/reduce_scatter | solution.py:54
  316.8 4.3 %copy.22 = f32[512,4,256]{2,1,0:T(4,128)} copy(f32[512,4,256]{2,0,1:T(8,128)} %reduce-scatter.2.cloned.1.call-done) | data formatting | bytes 4194304 | tf_op jit(solution)/shard_map/reduce_scatter | solution.py:54
  321.1 0.0 copy-done.1
  (5 shorter events, 0.0 us)
Async XLA Ops:
  6.5 9.4 %copy-start = (bf16[1,8,64,3072]{3,2,1,0:T(8,128)(2,1)S(1)}, bf16[1,8,64,3072]{3,2,1,0:T(8,128)(2,1)}, u32[]{:S(2)}) copy-start(bf16[1,8,64,3072]{3,2,1,0:T(8,128)(2,1)} %param.4) | copy-start | bytes 9437188
  6.5 190.0 %all-gather.2.cloned.1.call-start = ((), (), s32[]{:S(2)}) async-start(), calls=%async_computation.1 | async-start | bytes 26738688 | tf_op jit(solution)/shard_map/all_gather | solution.py:45
  57.5 259.3 %reduce-scatter.2.cloned.1.call-start = ((), (), s32[]{:S(2)}) async-start(), calls=%async_computation.2 | async-start | bytes 6291456 | tf_op jit(solution)/shard_map/reduce_scatter | solution.py:54
  252.5 68.6 %copy-start.1 = (bf16[1,8,64,3072]{3,2,1,0:T(8,128)(2,1)S(1)}, bf16[1,8,64,3072]{3,2,1,0:T(8,128)(2,1)}, u32[]{:S(2)}) copy-start(bf16[1,8,64,3072]{3,2,1,0:T(8,128)(2,1)} %param.4) | copy-start | bytes 9437188
Sparse Core Ops, SparseCore 0:
  57.6 138.8 all-gather.1
  263.0 53.7 reduce-scatter.1
where the time goes:
time: 332 us; the launch traced here: 328 us
  waiting for transfers between devices  193 us (58%)
  local copies, waits for them, and re-layouts  84.7 us (26%)
  matrix products  35.8 us (11%)
  between operations  13.5 us (4%)
    all_gather x1, waiting for transfers between devices, local(): gathered = lax.all_gather(half_local, ('row', 'col'), axis=2, tiled=True)  139 us
    reduce_scatter x1, waiting for transfers between devices, local(): lax.psum_scatter(exchange_tile, 'aux', scatter_dimension=0, tiled=True)  53.9 us
    reshape x1, local copies, waits for them, and re-layouts, local(): gathered.reshape(occ_count, aux_count, row_count, col_count, local_rows)  41.3 us
    dot_general x1, matrix products, half_transform(): jnp.einsum('sb,siqm->iqbm', weights, products, precision=lax.Precision.HI...  21.8 us
    dynamic_slice x1, local copies, waits for them, and re-layouts, local(): lax.dynamic_index_in_dim(grid_view, col_index, 3, keepdims=False)  14.7 us
    dot_general x1, matrix products, local(): lax.dot_general(rows_panel, column_panel, contract, preferred_element_typ...  10.4 us
    reshape x1, local copies, waits for them, and re-layouts, half_transform(): products = products.reshape(capacity, occ_count, aux_count, block_size)  9.96 us
  transfers between devices with their start and end apart: 2, of which 2 were waited for; matrix products, arithmetic and copies ran while one was open for 0% of the time, Pallas kernels for 0%

commit v1 on v0

v1 whole, which is shorter than its diff:
```python
import functools

import jax
import jax.numpy as jnp
from jax import lax
from jax.experimental import pallas as pl
from jax.experimental.pallas import tpu as pltpu
from jax.sharding import PartitionSpec as P

MESH = pl.DeviceIdType.MESH
LANES = 128


def weigh(dims, mask_ref, slot_ref, orb_ref, weights):
    MB, OCC, BLK, CAP = dims
    mask, slot = mask_ref[...], slot_ref[...]
    lane_count = mask.shape[1]
    row_ids = lax.broadcasted_iota(jnp.int32, mask.shape, 0)
    lam_ids = lax.broadcasted_iota(jnp.int32, mask.shape, 1)
    code = row_ids * lane_count + lam_ids
    low = lax.broadcasted_iota(jnp.int32, (OCC, LANES), 1) < BLK

    def slot_block(s, half):
        select = jnp.where((mask == 1) & (slot == s), 1, 0)
        position = jnp.sum(select * (code + 1))
        present = jnp.minimum(position, 1)
        place = jnp.maximum(position - 1, 0)
        lam, row = place % lane_count, place // lane_count
        start = pl.multiple_of((lam // 2) * LANES, LANES)
        values = orb_ref[:, pl.ds(start, LANES)].astype(jnp.float32)
        odd = lam % 2
        values = jnp.where(odd == half, values, pltpu.roll(values, BLK, 1))
        return values, row, present

    for p in range(CAP // 2):
        lo, lo_row, lo_here = slot_block(2 * p, 0)
        hi, hi_row, hi_here = slot_block(2 * p + 1, 1)
        for b in range(MB):
            lo_w = jnp.where(lo_row == b, lo_here, 0).astype(jnp.float32)
            hi_w = jnp.where(hi_row == b, hi_here, 0).astype(jnp.float32)
            weights[b * OCC : (b + 1) * OCC, p * LANES : (p + 1) * LANES] = jnp.where(
                low, lo * lo_w, hi * hi_w
            ).astype(jnp.bfloat16)


def kernel(
    dims,
    packed_ref,
    weights,
    out_ref,
    panel,
    column,
    block,
    kept,
    send_sum,
    send_turn,
    recv_sum,
    recv_turn,
    z_recv,
    z_up,
    z_down,
    row_recv,
    row_send,
    sum_send,
    sum_recv,
    turn_send,
    turn_recv,
):
    R, C, A, MB, OCC, BLK, CAP, KDIM, PIECES = dims
    T = MB * BLK
    NH = T // LANES
    NT = C // A
    half_c = C // 2
    step = KDIM // PIECES
    r, c, a = lax.axis_index("row"), lax.axis_index("col"), lax.axis_index("aux")
    devices = R * C * A
    me = (r * C + c) * A + a

    barrier = pltpu.get_barrier_semaphore()

    def greet(k, _):
        @pl.when(k != me)
        def _():
            pl.semaphore_signal(
                barrier,
                inc=1,
                device_id={"row": k // (C * A), "col": (k // A) % C, "aux": k % A},
                device_id_type=MESH,
            )

        return 0

    lax.fori_loop(0, devices, greet, 0)

    low = lax.broadcasted_iota(jnp.int32, (OCC, LANES), 1) < BLK

    def transform(g, _):
        at = pl.multiple_of(g * 256, 256)
        h = jnp.dot(
            weights[...], packed_ref[:, pl.ds(at, 256)], preferred_element_type=jnp.float32
        )
        for j in range(2):
            for hh in range(NH):
                b0 = h[2 * hh * OCC : (2 * hh + 1) * OCC, j * LANES : (j + 1) * LANES]
                b1 = h[(2 * hh + 1) * OCC : (2 * hh + 2) * OCC, j * LANES : (j + 1) * LANES]
                even = jnp.where(low, b0, pltpu.roll(b1, BLK, 1)).astype(jnp.bfloat16)
                odd = jnp.where(low, pltpu.roll(b0, BLK, 1), b1).astype(jnp.bfloat16)
                first = pl.multiple_of((g * 4 + 2 * j) * OCC, OCC)
                second = pl.multiple_of((g * 4 + 2 * j + 1) * OCC, OCC)
                lanes = slice(hh * LANES, (hh + 1) * LANES)
                panel[c, hh, pl.ds(first, OCC), :] = even
                panel[c, hh, pl.ds(second, OCC), :] = odd
                column[r, pl.ds(first, OCC), lanes] = even
                column[r, pl.ds(second, OCC), lanes] = odd
        return 0

    lax.fori_loop(0, KDIM // 256, transform, 0)

    pl.semaphore_wait(barrier, devices - 1)

    def z_copy(src, hh, p, up):
        ref = panel.at[src, hh, pl.ds(pl.multiple_of(p * step, step), step), :]
        target = jnp.minimum(c + 1, C - 1) if up else jnp.maximum(c - 1, 0)
        index = (src * NH + hh) * PIECES + p
        return pltpu.make_async_remote_copy(
            src_ref=ref,
            dst_ref=ref,
            send_sem=(z_up if up else z_down).at[index],
            recv_sem=z_recv.at[index],
            device_id={"row": r, "col": target, "aux": a},
            device_id_type=MESH,
        )

    def row_copy(tile, target, send_index):
        return pltpu.make_async_remote_copy(
            src_ref=column.at[tile],
            dst_ref=column.at[tile],
            send_sem=row_send.at[send_index],
            recv_sem=row_recv.at[tile],
            device_id={"row": target, "col": c, "aux": a},
            device_id_type=MESH,
        )

    def each_piece(act):
        lax.fori_loop(0, PIECES, lambda p, _: (act(p), 0)[1], 0)

    sends_up = (c < half_c) & (c + 1 < C)
    sends_down = c - 1 >= half_c
    sibling = r + 1 - 2 * (r % 2)
    pairs = R // 2
    peers = [(r + 2 * j) % R for j in range(pairs)]
    far = [(sibling + 2 * j) % R for j in range(pairs)]

    for j in range(1, pairs):
        row_copy(r, peers[j], j).start()
    row_copy(r, sibling, 0).start()
    for hh in range(NH):

        @pl.when(sends_up)
        def _():
            each_piece(lambda p: z_copy(c, hh, p, True).start())

        @pl.when(sends_down)
        def _():
            each_piece(lambda p: z_copy(c, hh, p, False).start())

    def has_up(src):
        return (src >= 0) & (src < half_c)

    def has_down(src):
        return (src < C) & (c >= half_c)

    def take(src, hh, p, up):
        z_copy(src, hh, p, up).wait_recv()

        @pl.when((c + 1 < C) if up else (c - 1 >= half_c))
        def _():
            z_copy(src, hh, p, up).start()

    for hh in range(NH):

        @pl.when(has_up(c - 1))
        def _():
            each_piece(lambda p: take(c - 1, hh, p, True))

    for j in range(1, pairs):
        row_copy(peers[j], sibling, j).wait_recv()
        row_copy(peers[j], sibling, pairs + j).start()
    for j in range(pairs):
        row_copy(far[j], sibling, 0).wait_recv()

    def sum_copy(src, hh):
        return pltpu.make_async_remote_copy(
            src_ref=send_sum.at[src, hh],
            dst_ref=recv_sum.at[src % NT, a, hh],
            send_sem=sum_send.at[src * NH + hh],
            recv_sem=sum_recv.at[((src % NT) * A + a) * NH + hh],
            device_id={"row": r, "col": c, "aux": src // NT},
            device_id_type=MESH,
        )

    def turn_copy(src, hh, r2):
        return pltpu.make_async_remote_copy(
            src_ref=send_turn.at[src, hh, r2],
            dst_ref=recv_turn.at[c % NT, a, r, hh],
            send_sem=turn_send.at[(src * NH + hh) * R + r2],
            recv_sem=turn_recv.at[(((c % NT) * A + a) * R + r) * NH + hh],
            device_id={"row": r2, "col": src, "aux": c // NT},
            device_id_type=MESH,
        )

    def multiply(src, hh, p, r2):
        rows = pl.ds(pl.multiple_of(p * step, step), step)
        return lax.dot_general(
            panel[src, hh, rows, :],
            column[r2, rows, :],
            (((0,), (0,)), ((), ())),
            preferred_element_type=jnp.float32,
        )

    def product(src, hh, before, turned):
        def piece(p, _):
            before(p)

            def one(r2, _):
                value = multiply(src, hh, p, r2)
                block[r2] = jnp.where(p == 0, value, block[r2] + value)
                return 0

            return lax.fori_loop(0, R, one, 0)

        lax.fori_loop(0, PIECES, piece, 0)

        if turned:

            def turn(r2, _):
                send_turn[src, hh, r2] = block[r2].T.astype(jnp.bfloat16)
                turn_copy(src, hh, r2).start()
                return 0

            lax.fori_loop(0, R, turn, 0)

        @pl.when(src // NT == a)
        def _():
            kept[src % NT, hh] = block[...]

        @pl.when(src // NT != a)
        def _():
            send_sum[src, hh] = block[...].astype(jnp.bfloat16)
            sum_copy(src, hh).start()

    block[...] = jnp.zeros_like(block)
    for hh in range(NH):
        product(c, hh, lambda p: None, False)
    for d in range(1, C):
        for hh in range(NH):

            @pl.when(has_up(c - d))
            def _():
                before = (lambda p: None) if d == 1 else lambda p: take(c - d, hh, p, True)
                product(c - d, hh, before, True)

            @pl.when(has_down(c + d))
            def _():
                product(c + d, hh, lambda p: take(c + d, hh, p, False), True)

    for t in range(NT):
        tile = a * NT + t
        here = (tile == c) | ((tile < c) & (tile < half_c)) | ((tile > c) & (c >= half_c))

        @pl.when(here)
        def _():
            for hh in range(NH):

                def add(other, _):
                    source = (a + other) % A
                    index = (t * A + source) * NH + hh
                    pltpu.make_async_remote_copy(
                        src_ref=recv_sum.at[t, source, hh],
                        dst_ref=recv_sum.at[t, source, hh],
                        send_sem=sum_send.at[0],
                        recv_sem=sum_recv.at[index],
                        device_id={"row": r, "col": c, "aux": source},
                        device_id_type=MESH,
                    ).wait_recv()
                    kept[t, hh] = kept[t, hh] + recv_sum[t, source, hh].astype(jnp.float32)
                    return 0

                lax.fori_loop(1, A, add, 0)
                for r2 in range(R):
                    out_ref[
                        t * T + hh * LANES : t * T + (hh + 1) * LANES, r2 * T : (r2 + 1) * T
                    ] = kept[t, hh, r2]

        @pl.when(jnp.logical_not(here))
        def _():
            for hh in range(NH):
                for r2 in range(R):

                    def add(source, total):
                        index = ((t * A + source) * R + r2) * NH + hh
                        pltpu.make_async_remote_copy(
                            src_ref=recv_turn.at[t, source, r2, hh],
                            dst_ref=recv_turn.at[t, source, r2, hh],
                            send_sem=turn_send.at[0],
                            recv_sem=turn_recv.at[index],
                            device_id={"row": r2, "col": tile, "aux": source},
                            device_id_type=MESH,
                        ).wait_recv()
                        return total + recv_turn[t, source, r2, hh].astype(jnp.float32)

                    out_ref[
                        t * T : (t + 1) * T, r2 * T + hh * LANES : r2 * T + (hh + 1) * LANES
                    ] = lax.fori_loop(0, A, add, jnp.zeros((T, LANES), jnp.float32))

    for j in range(1, pairs):
        row_copy(r, peers[j], j).wait_send()
        row_copy(peers[j], sibling, pairs + j).wait_send()
    row_copy(r, sibling, 0).wait_send()
    for hh in range(NH):

        @pl.when(sends_up)
        def _():
            each_piece(lambda p: z_copy(c, hh, p, True).wait_send())

        @pl.when(sends_down)
        def _():
            each_piece(lambda p: z_copy(c, hh, p, False).wait_send())

    def finish(src, hh, up, turned):
        if turned:

            @pl.when((c + 1 < C) if up else (c - 1 >= half_c))
            def _():
                each_piece(lambda p: z_copy(src, hh, p, up).wait_send())

            lax.fori_loop(0, R, lambda r2, _: (turn_copy(src, hh, r2).wait_send(), 0)[1], 0)

        @pl.when(src // NT != a)
        def _():
            sum_copy(src, hh).wait_send()

    for hh in range(NH):
        finish(c, hh, True, False)
    for d in range(1, C):
        for hh in range(NH):

            @pl.when(has_up(c - d))
            def _():
                finish(c - d, hh, True, True)

            @pl.when(has_down(c + d))
            def _():
                finish(c + d, hh, False, True)


def local(sizes, integrals, block_mask, block_slots, orbitals):
    R, C, A = sizes
    _, cap, blk, width = integrals.shape
    mb = block_mask.shape[1]
    occ = orbitals.shape[0]
    T = mb * blk
    kdim = occ * (width // blk)
    NH, NT, pieces = T // LANES, C // A, 4
    dims = (R, C, A, mb, occ, blk, cap, kdim, pieces)
    dma = pltpu.SemaphoreType.DMA
    bf16, f32 = jnp.bfloat16, jnp.float32
    vmem = pl.BlockSpec(memory_space=pltpu.VMEM)
    weights = pl.pallas_call(
        functools.partial(weigh, (mb, occ, blk, cap)),
        out_shape=jax.ShapeDtypeStruct((mb * occ, cap * blk), bf16),
        in_specs=[vmem] * 3,
        out_specs=vmem,
    )(
        block_mask.reshape(block_mask.shape[1:]),
        block_slots.reshape(block_slots.shape[1:]),
        orbitals,
    )
    result = pl.pallas_call(
        functools.partial(kernel, dims),
        out_shape=jax.ShapeDtypeStruct((NT * T, R * T), f32),
        in_specs=[vmem] * 2,
        out_specs=vmem,
        scratch_shapes=[
            pltpu.VMEM((C, NH, kdim, LANES), bf16),
            pltpu.VMEM((R, kdim, T), bf16),
            pltpu.VMEM((R, LANES, T), f32),
            pltpu.VMEM((NT, NH, R, LANES, T), f32),
            pltpu.VMEM((C, NH, R, LANES, T), bf16),
            pltpu.VMEM((C, NH, R, T, LANES), bf16),
            pltpu.VMEM((NT, A, NH, R, LANES, T), bf16),
            pltpu.VMEM((NT, A, R, NH, T, LANES), bf16),
            dma((C * NH * pieces,)),
            dma((C * NH * pieces,)),
            dma((C * NH * pieces,)),
            dma((R,)),
            dma((R,)),
            dma((C * NH,)),
            dma((NT * A * NH,)),
            dma((C * NH * R,)),
            dma((NT * A * R * NH,)),
        ],
        compiler_params=pltpu.CompilerParams(
            collective_id=0, has_side_effects=True, vmem_limit_bytes=50 * 1024 * 1024
        ),
        cost_estimate=pl.CostEstimate(
            flops=2 * C * T * R * T * kdim, bytes_accessed=8 * 1024 * 1024, transcendentals=0
        ),
    )(
        integrals.reshape(cap * blk, width), weights
    )
    return result.reshape(NT * T, R, T)


def solution(mesh):
    sizes = tuple(mesh.shape[name] for name in ("row", "col", "aux"))
    placed = (
        P("aux", ("row", "col"), None, None),
        P("aux", ("row", "col"), None),
        P("aux", ("row", "col"), None),
        P(),
    )
    return jax.shard_map(
        functools.partial(local, sizes),
        mesh=mesh,
        in_specs=placed,
        out_specs=P(("row", "aux"), None, "col"),
        check_vma=False,
    )
```

time: 332 us -> 133 us (0.40); the launches traced: 328 us -> 133 us
  waiting for transfers between devices: 193 us -> 0 us
  Pallas kernels: 0 us -> 130 us
  local copies, waits for them, and re-layouts: 84.7 us -> 2.94 us
  matrix products: 35.8 us -> 0 us
  between operations: 13.5 us -> 0.01 us
    all_gather x1 -> x0, waiting for transfers between devices: 139 us -> none  [local(): gathered = lax.all_gather(half_local, ('row', 'col'), axis=2, tiled=True)]
    pallas_call x0 -> x2, Pallas kernels: none -> 130 us  [the longest x1 128 us: local(): pl.pallas_call(functools.partial(kernel, dims), out_shape=jax.ShapeDtypeS...]
    reshape x4 -> x1, local copies, waits for them, and re-layouts: 56.9 us -> 1.99 us  [local(): return result.reshape(NT * T, R, T)]
    reduce_scatter x1 -> x0, waiting for transfers between devices: 53.9 us -> none  [local(): lax.psum_scatter(exchange_tile, 'aux', scatter_dimension=0, tiled=True)]
    dot_general x3 -> x0, matrix products: 35.8 us -> none  [the longest x1 21.8 us: half_transform(): jnp.einsum('sb,siqm->iqbm', weights, products, precision=lax.Precision.HI...]
    dynamic_slice x1 -> x0, local copies, waits for them, and re-layouts: 14.7 us -> none  [local(): lax.dynamic_index_in_dim(grid_view, col_index, 3, keepdims=False)]
    convert_element_type x2 -> x0, local copies, waits for them, and re-layouts: 6.13 us -> none  [half_transform(): half_block.reshape(occ_count, aux_count, row_blocks * block_size)]
    reduce_scatter x1 -> x0, local copies, waits for them, and re-layouts: 4.26 us -> none  [local(): lax.psum_scatter(exchange_tile, 'aux', scatter_dimension=0, tiled=True)]
  transfers between devices with their start and end apart: 2 -> 0, of which waited for: 2 -> 0; matrix products, arithmetic and copies ran while one was open for 0% -> 0% of each run, Pallas kernels for 0% -> 0%
where the time goes in v1:
time: 133 us
  Pallas kernels  130 us (98%)
  local copies, waits for them, and re-layouts  2.94 us (2%)
    pallas_call x1, Pallas kernels, local(): pl.pallas_call(functools.partial(kernel, dims), out_shape=jax.ShapeDtypeS...  128 us

profile of v1, /device:TPU:7, one launch (start us, length us, event | category | flops | bytes accessed | tf_op | source)
XLA Modules:
  0.0 132.6 jit_solution(17418145045268213208)
XLA Ops:
  0.0 2.1 %shard_map.46.weights = bf16[256,512]{1,0:T(8,128)(2,1)} custom-call(s32[4,64]{1,0:T(4,128)} %bitcast.3, s32[4,64]{1,0:T(4,128)} %bitcast.4, bf16[64,4096]{1,0:T(8,128)(2,1)} %orb_ref.1), custom_call_target="tpu_custom_call" | custom-call | tf_op jit(solution)/shard_map/pallas_call | solution.py:369
  2.1 0.0 copy-start
  2.1 0.9 copy-done
  3.1 127.6 %shard_map.47 = f32[512,1024]{1,0:T(8,128)S(1)} custom-call(bf16[512,3072]{1,0:T(8,128)(2,1)} %bitcast.5, bf16[256,512]{1,0:T(8,128)(2,1)S(1)} %copy-done), custom_call_target="tpu_custom_call" | custom-call | flops 6442450944 | bytes 8388608 | tf_op jit(solution)/shard_map/pallas_call | solution.py:379
  130.6 2.0 %reshape.15 = f32[512,4,256]{2,1,0:T(4,128)} reshape(f32[512,1024]{1,0:T(8,128)S(1)} %shard_map.47) | data formatting | bytes 4194304 | tf_op jit(solution)/shard_map/reshape | solution.py:412
Async XLA Ops:
  2.1 0.9 copy-start

commit v2 on v1

--- a/solution.py
+++ b/solution.py
@@ -52,8 +52,7 @@
     column,
     block,
     kept,
-    send_sum,
-    send_turn,
+    send,
     recv_sum,
     recv_turn,
     z_recv,
@@ -99,19 +98,16 @@
         h = jnp.dot(
             weights[...], packed_ref[:, pl.ds(at, 256)], preferred_element_type=jnp.float32
         )
-        for j in range(2):
-            for hh in range(NH):
+        for hh in range(NH):
+            parts = []
+            for j in range(2):
                 b0 = h[2 * hh * OCC : (2 * hh + 1) * OCC, j * LANES : (j + 1) * LANES]
                 b1 = h[(2 * hh + 1) * OCC : (2 * hh + 2) * OCC, j * LANES : (j + 1) * LANES]
-                even = jnp.where(low, b0, pltpu.roll(b1, BLK, 1)).astype(jnp.bfloat16)
-                odd = jnp.where(low, pltpu.roll(b0, BLK, 1), b1).astype(jnp.bfloat16)
-                first = pl.multiple_of((g * 4 + 2 * j) * OCC, OCC)
-                second = pl.multiple_of((g * 4 + 2 * j + 1) * OCC, OCC)
-                lanes = slice(hh * LANES, (hh + 1) * LANES)
-                panel[c, hh, pl.ds(first, OCC), :] = even
-                panel[c, hh, pl.ds(second, OCC), :] = odd
-                column[r, pl.ds(first, OCC), lanes] = even
-                column[r, pl.ds(second, OCC), lanes] = odd
+                parts.append(jnp.where(low, b0, pltpu.roll(b1, BLK, 1)))
+                parts.append(jnp.where(low, pltpu.roll(b0, BLK, 1), b1))
+            tile = jnp.concatenate(parts, axis=0)
+            panel[c, hh, pl.ds(at, 256), :] = tile.astype(jnp.bfloat16)
+            column[r, hh * LANES : (hh + 1) * LANES, pl.ds(at, 256)] = tile.T.astype(jnp.bfloat16)
         return 0
 
     lax.fori_loop(0, KDIM // 256, transform, 0)
@@ -177,11 +173,16 @@
         def _():
             z_copy(src, hh, p, up).start()
 
+    passes_down = c - 1 >= half_c
     for hh in range(NH):
 
         @pl.when(has_up(c - 1))
         def _():
             each_piece(lambda p: take(c - 1, hh, p, True))
+
+        @pl.when(has_down(c + 1) & passes_down)
+        def _():
+            each_piece(lambda p: take(c + 1, hh, p, False))
 
     for j in range(1, pairs):
         row_copy(peers[j], sibling, j).wait_recv()
@@ -191,7 +192,7 @@
 
     def sum_copy(src, hh):
         return pltpu.make_async_remote_copy(
-            src_ref=send_sum.at[src, hh],
+            src_ref=send.at[src, hh],
             dst_ref=recv_sum.at[src % NT, a, hh],
             send_sem=sum_send.at[src * NH + hh],
             recv_sem=sum_recv.at[((src % NT) * A + a) * NH + hh],
@@ -201,7 +202,7 @@
 
     def turn_copy(src, hh, r2):
         return pltpu.make_async_remote_copy(
-            src_ref=send_turn.at[src, hh, r2],
+            src_ref=send.at[src, hh, r2],
             dst_ref=recv_turn.at[c % NT, a, r, hh],
             send_sem=turn_send.at[(src * NH + hh) * R + r2],
             recv_sem=turn_recv.at[(((c % NT) * A + a) * R + r) * NH + hh],
@@ -209,60 +210,87 @@
             device_id_type=MESH,
         )
 
-    def multiply(src, hh, p, r2):
-        rows = pl.ds(pl.multiple_of(p * step, step), step)
-        return lax.dot_general(
-            panel[src, hh, rows, :],
-            column[r2, rows, :],
-            (((0,), (0,)), ((), ())),
-            preferred_element_type=jnp.float32,
-        )
-
-    def product(src, hh, before, turned):
+    def settle(src, hh, r2, value, turned):
+        send[src, hh, r2] = value.astype(jnp.bfloat16)
+        if turned:
+            turn_copy(src, hh, r2).start()
+
+        @pl.when(src // NT == a)
+        def _():
+            kept[src % NT, hh, r2] = value
+
+    def pass_sum(src, hh):
+        @pl.when(src // NT != a)
+        def _():
+            sum_copy(src, hh).start()
+
+    def whole(src, turned):
+        def one(r2, _):
+            tile = jnp.concatenate([panel[src, hh] for hh in range(NH)], axis=1)
+            value = jnp.dot(column[r2], tile, preferred_element_type=jnp.float32)
+            for hh in range(NH):
+                settle(src, hh, r2, value[:, hh * LANES : (hh + 1) * LANES], turned)
+            return 0
+
+        lax.fori_loop(0, R, one, 0)
+        for hh in range(NH):
+            pass_sum(src, hh)
+
+    def streamed(src, hh, up):
         def piece(p, _):
-            before(p)
-
-            def one(r2, _):
-                value = multiply(src, hh, p, r2)
+            take(src, hh, p, up)
+            rows = pl.ds(pl.multiple_of(p * step, step), step)
+            for r2 in range(R):
+                value = jnp.dot(
+                    column[r2, :, rows],
+                    panel[src, hh, rows, :],
+                    preferred_element_type=jnp.float32,
+                )
                 block[r2] = jnp.where(p == 0, value, block[r2] + value)
-                return 0
-
-            return lax.fori_loop(0, R, one, 0)
+            return 0
 
         lax.fori_loop(0, PIECES, piece, 0)
 
-        if turned:
-
-            def turn(r2, _):
-                send_turn[src, hh, r2] = block[r2].T.astype(jnp.bfloat16)
-                turn_copy(src, hh, r2).start()
-                return 0
-
-            lax.fori_loop(0, R, turn, 0)
-
-        @pl.when(src // NT == a)
-        def _():
-            kept[src % NT, hh] = block[...]
-
-        @pl.when(src // NT != a)
-        def _():
-            send_sum[src, hh] = block[...].astype(jnp.bfloat16)
-            sum_copy(src, hh).start()
+        def one(r2, _):
+            settle(src, hh, r2, block[r2], True)
+            return 0
+
+        lax.fori_loop(0, R, one, 0)
+        pass_sum(src, hh)
 
     block[...] = jnp.zeros_like(block)
-    for hh in range(NH):
-        product(c, hh, lambda p: None, False)
-    for d in range(1, C):
+    whole(c, False)
+
+    @pl.when(has_up(c - 1))
+    def _():
+        whole(c - 1, True)
+
+    def nearest_down():
+        @pl.when(has_down(c + 1))
+        def _():
+            @pl.when(jnp.logical_not(passes_down))
+            def _():
+                for hh in range(NH):
+                    each_piece(lambda p: z_copy(c + 1, hh, p, False).wait_recv())
+
+            whole(c + 1, True)
+
+    for d in range(2, C):
         for hh in range(NH):
 
             @pl.when(has_up(c - d))
             def _():
-                before = (lambda p: None) if d == 1 else lambda p: take(c - d, hh, p, True)
-                product(c - d, hh, before, True)
+                streamed(c - d, hh, True)
+
+            if d == 2 and hh == 0:
+                nearest_down()
 
             @pl.when(has_down(c + d))
             def _():
-                product(c + d, hh, lambda p: take(c + d, hh, p, False), True)
+                streamed(c + d, hh, False)
+
+    if C == 2:
+        nearest_down()
 
     for t in range(NT):
         tile = a * NT + t
@@ -272,7 +300,7 @@
         def _():
             for hh in range(NH):
 
-                def add(other, _):
+                def arrived(other, _):
                     source = (a + other) % A
                     index = (t * A + source) * NH + hh
                     pltpu.make_async_remote_copy(
@@ -286,11 +314,11 @@
                     kept[t, hh] = kept[t, hh] + recv_sum[t, source, hh].astype(jnp.float32)
                     return 0
 
-                lax.fori_loop(1, A, add, 0)
+                lax.fori_loop(1, A, arrived, 0)
                 for r2 in range(R):
                     out_ref[
                         t * T + hh * LANES : t * T + (hh + 1) * LANES, r2 * T : (r2 + 1) * T
-                    ] = kept[t, hh, r2]
+                    ] = kept[t, hh, r2].T
 
         @pl.when(jnp.logical_not(here))
         def _():
@@ -383,12 +411,11 @@
         out_specs=vmem,
         scratch_shapes=[
             pltpu.VMEM((C, NH, kdim, LANES), bf16),
-            pltpu.VMEM((R, kdim, T), bf16),
-            pltpu.VMEM((R, LANES, T), f32),
-            pltpu.VMEM((NT, NH, R, LANES, T), f32),
-            pltpu.VMEM((C, NH, R, LANES, T), bf16),
+            pltpu.VMEM((R, T, kdim), bf16),
+            pltpu.VMEM((R, T, LANES), f32),
+            pltpu.VMEM((NT, NH, R, T, LANES), f32),
             pltpu.VMEM((C, NH, R, T, LANES), bf16),
-            pltpu.VMEM((NT, A, NH, R, LANES, T), bf16),
+            pltpu.VMEM((NT, A, NH, R, T, LANES), bf16),
             pltpu.VMEM((NT, A, R, NH, T, LANES), bf16),
             dma((C * NH * pieces,)),
             dma((C * NH * pieces,)),

time: 133 us -> 120 us (0.902)
  Pallas kernels: 130 us -> 117 us
    pallas_call x1, Pallas kernels: 128 us -> 114 us  [local(): pl.pallas_call(functools.partial(kernel, dims), out_shape=jax.ShapeDtypeS...]
where the time goes in v2:
time: 120 us; the launch traced here: 119 us
  Pallas kernels  117 us (98%)
  local copies, waits for them, and re-layouts  2.94 us (2%)
    pallas_call x1, Pallas kernels, local(): pl.pallas_call(functools.partial(kernel, dims), out_shape=jax.ShapeDtypeS...  114 us

profile of v2, /device:TPU:7, one launch (start us, length us, event | category | flops | bytes accessed | tf_op | source)
XLA Modules:
  0.0 119.5 jit_solution(9598959607253900545)
XLA Ops:
  0.0 2.1 %shard_map.46.weights = bf16[256,512]{1,0:T(8,128)(2,1)} custom-call(s32[4,64]{1,0:T(4,128)} %bitcast.3, s32[4,64]{1,0:T(4,128)} %bitcast.4, bf16[64,4096]{1,0:T(8,128)(2,1)} %orb_ref.1), custom_call_target="tpu_custom_call" | custom-call | tf_op jit(solution)/shard_map/pallas_call | solution.py:397
  2.1 0.0 copy-start
  2.1 0.9 copy-done
  3.1 114.4 %shard_map.47 = f32[512,1024]{1,0:T(8,128)S(1)} custom-call(bf16[512,3072]{1,0:T(8,128)(2,1)} %bitcast.5, bf16[256,512]{1,0:T(8,128)(2,1)S(1)} %copy-done), custom_call_target="tpu_custom_call" | custom-call | flops 6442450944 | bytes 8388608 | tf_op jit(solution)/shard_map/pallas_call | solution.py:407
  117.5 2.0 %reshape.15 = f32[512,4,256]{2,1,0:T(4,128)} reshape(f32[512,1024]{1,0:T(8,128)S(1)} %shard_map.47) | data formatting | bytes 4194304 | tf_op jit(solution)/shard_map/reshape | solution.py:439
Async XLA Ops:
  2.1 0.9 copy-start

commit v3 on v2

--- a/solution.py
+++ b/solution.py
@@ -45,16 +45,18 @@
 
 def kernel(
     dims,
-    packed_ref,
+    packed_hbm,
     weights,
     out_ref,
+    packed_ref,
     panel,
     column,
-    block,
     kept,
     send,
     recv_sum,
+    send_turn,
     recv_turn,
+    load,
     z_recv,
     z_up,
     z_down,
@@ -75,6 +77,8 @@
     devices = R * C * A
     me = (r * C + c) * A + a
 
+    loading = pltpu.make_async_copy(packed_hbm, packed_ref, load)
+    loading.start()
     barrier = pltpu.get_barrier_semaphore()
 
     def greet(k, _):
@@ -110,10 +114,6 @@
             column[r, hh * LANES : (hh + 1) * LANES, pl.ds(at, 256)] = tile.T.astype(jnp.bfloat16)
         return 0
 
-    lax.fori_loop(0, KDIM // 256, transform, 0)
-
-    pl.semaphore_wait(barrier, devices - 1)
-
     def z_copy(src, hh, p, up):
         ref = panel.at[src, hh, pl.ds(pl.multiple_of(p * step, step), step), :]
         target = jnp.minimum(c + 1, C - 1) if up else jnp.maximum(c - 1, 0)
@@ -147,18 +147,39 @@
     peers = [(r + 2 * j) % R for j in range(pairs)]
     far = [(sibling + 2 * j) % R for j in range(pairs)]
 
+    def send_own(hh, p):
+        @pl.when(sends_up)
+        def _():
+            z_copy(c, hh, p, True).start()
+
+        @pl.when(sends_down)
+        def _():
+            z_copy(c, hh, p, False).start()
+
+    edge = half_c - 1
+    loading.wait()
+    pl.semaphore_wait(barrier, devices - 1)
+
+    def make_piece(p, _):
+        lax.fori_loop(p * (step // 256), (p + 1) * (step // 256), transform, 0)
+        send_own(0, p)
+
+        @pl.when(c == edge)
+        def _():
+            for hh in range(1, NH):
+                send_own(hh, p)
+
+        return 0
+
+    lax.fori_loop(0, PIECES, make_piece, 0)
     for j in range(1, pairs):
         row_copy(r, peers[j], j).start()
     row_copy(r, sibling, 0).start()
-    for hh in range(NH):
-
-        @pl.when(sends_up)
-        def _():
-            each_piece(lambda p: z_copy(c, hh, p, True).start())
-
-        @pl.when(sends_down)
-        def _():
-            each_piece(lambda p: z_copy(c, hh, p, False).start())
+
+    @pl.when(c != edge)
+    def _():
+        for hh in range(1, NH):
+            each_piece(lambda p: send_own(hh, p))
 
     def has_up(src):
         return (src >= 0) & (src < half_c)
@@ -174,14 +195,21 @@
             z_copy(src, hh, p, up).start()
 
     passes_down = c - 1 >= half_c
-    for hh in range(NH):
-
-        @pl.when(has_up(c - 1))
-        def _():
-            each_piece(lambda p: take(c - 1, hh, p, True))
-
-        @pl.when(has_down(c + 1) & passes_down)
-        def _():
+
+    @pl.when(has_up(c - 1))
+    def _():
+        def one(n, _):
+            by_piece = c - 1 == edge
+            hh = jnp.where(by_piece, n % NH, n // PIECES)
+            p = jnp.where(by_piece, n // NH, n % PIECES)
+            take(c - 1, hh, p, True)
+            return 0
+
+        lax.fori_loop(0, NH * PIECES, one, 0)
+
+    @pl.when(has_down(c + 1) & passes_down)
+    def _():
+        for hh in range(NH):
             each_piece(lambda p: take(c + 1, hh, p, False))
 
     for j in range(1, pairs):
@@ -190,55 +218,64 @@
     for j in range(pairs):
         row_copy(far[j], sibling, 0).wait_recv()
 
-    def sum_copy(src, hh):
+    def sum_copy(src, hh, r2, other):
+        index = ((src * A + a) * NH + hh) * R + r2
         return pltpu.make_async_remote_copy(
-            src_ref=send.at[src, hh],
-            dst_ref=recv_sum.at[src % NT, a, hh],
-            send_sem=sum_send.at[src * NH + hh],
-            recv_sem=sum_recv.at[((src % NT) * A + a) * NH + hh],
-            device_id={"row": r, "col": c, "aux": src // NT},
+            src_ref=send.at[src, hh, r2],
+            dst_ref=recv_sum.at[src, a, hh, r2],
+            send_sem=sum_send.at[((src * A + other) * NH + hh) * R + r2],
+            recv_sem=sum_recv.at[index],
+            device_id={"row": r, "col": c, "aux": other},
             device_id_type=MESH,
         )
 
     def turn_copy(src, hh, r2):
         return pltpu.make_async_remote_copy(
-            src_ref=send.at[src, hh, r2],
-            dst_ref=recv_turn.at[c % NT, a, r, hh],
+            src_ref=send_turn.at[src, hh, r2],
+            dst_ref=recv_turn.at[c % NT, r, hh],
             send_sem=turn_send.at[(src * NH + hh) * R + r2],
-            recv_sem=turn_recv.at[(((c % NT) * A + a) * R + r) * NH + hh],
-            device_id={"row": r2, "col": src, "aux": c // NT},
+            recv_sem=turn_recv.at[((c % NT) * R + r) * NH + hh],
+            device_id={"row": r2, "col": src, "aux": a},
             device_id_type=MESH,
         )
 
-    def settle(src, hh, r2, value, turned):
-        send[src, hh, r2] = value.astype(jnp.bfloat16)
-        if turned:
-            turn_copy(src, hh, r2).start()
-
-        @pl.when(src // NT == a)
-        def _():
-            kept[src % NT, hh, r2] = value
-
-    def pass_sum(src, hh):
-        @pl.when(src // NT != a)
-        def _():
-            sum_copy(src, hh).start()
+    def needs(src, turned, plane):
+        keeps = src // NT == plane
+        return keeps | (c // NT == plane) if turned else keeps
+
+    def each_other(src, turned, act):
+        def one(k, _):
+            other = (a + k) % A
+
+            @pl.when(needs(src, turned, other))
+            def _():
+                act(other)
+
+            return 0
+
+        lax.fori_loop(1, A, one, 0)
+
+    def share(src, hh, r2, turned):
+        send[src, hh, r2] = kept[src, hh, r2].astype(jnp.bfloat16)
+        each_other(src, turned, lambda other: sum_copy(src, hh, r2, other).start())
 
     def whole(src, turned):
         def one(r2, _):
             tile = jnp.concatenate([panel[src, hh] for hh in range(NH)], axis=1)
             value = jnp.dot(column[r2], tile, preferred_element_type=jnp.float32)
             for hh in range(NH):
-                settle(src, hh, r2, value[:, hh * LANES : (hh + 1) * LANES], turned)
+                kept[src, hh, r2] = value[:, hh * LANES : (hh + 1) * LANES]
+                share(src, hh, r2, turned)
             return 0
 
         lax.fori_loop(0, R, one, 0)
-        for hh in range(NH):
-            pass_sum(src, hh)
-
-    def streamed(src, hh, up):
+
+    def streamed(src, hh, up, taken=0):
         def piece(p, _):
-            take(src, hh, p, up)
+            @pl.when(p >= taken)
+            def _():
+                take(src, hh, p, up)
+
             rows = pl.ds(pl.multiple_of(p * step, step), step)
             for r2 in range(R):
                 value = jnp.dot(
@@ -246,51 +283,100 @@
                     panel[src, hh, rows, :],
                     preferred_element_type=jnp.float32,
                 )
-                block[r2] = jnp.where(p == 0, value, block[r2] + value)
+                kept[src, hh, r2] = jnp.where(p == 0, value, kept[src, hh, r2] + value)
             return 0
 
         lax.fori_loop(0, PIECES, piece, 0)
-
-        def one(r2, _):
-            settle(src, hh, r2, block[r2], True)
-            return 0
-
-        lax.fori_loop(0, R, one, 0)
-        pass_sum(src, hh)
-
-    block[...] = jnp.zeros_like(block)
+        lax.fori_loop(0, R, lambda r2, _: (share(src, hh, r2, True), 0)[1], 0)
+
+    def settle(src, hh, turned):
+        @pl.when(needs(src, turned, a))
+        def _():
+            def one(r2, _):
+                def add(k, total):
+                    other = (a + k) % A
+                    pltpu.make_async_remote_copy(
+                        src_ref=recv_sum.at[src, other, hh, r2],
+                        dst_ref=recv_sum.at[src, other, hh, r2],
+                        send_sem=sum_send.at[0],
+                        recv_sem=sum_recv.at[((src * A + other) * NH + hh) * R + r2],
+                        device_id={"row": r, "col": c, "aux": other},
+                        device_id_type=MESH,
+                    ).wait_recv()
+                    return total + recv_sum[src, other, hh, r2].astype(jnp.float32)
+
+                total = lax.fori_loop(1, A, add, kept[src, hh, r2])
+                kept[src, hh, r2] = total
+                if turned:
+
+                    @pl.when(c // NT == a)
+                    def _():
+                        send_turn[src, hh, r2] = total.astype(jnp.bfloat16)
+                        turn_copy(src, hh, r2).start()
+
+                return 0
+
+            lax.fori_loop(0, R, one, 0)
+
+    def settle_whole(src, turned):
+        for hh in range(NH):
+            settle(src, hh, turned)
+
+    def ahead(p):
+        if C > 2:
+
+            @pl.when(has_up(c - 2))
+            def _():
+                take(c - 2, 0, p, True)
+
     whole(c, False)
+    ahead(0)
 
     @pl.when(has_up(c - 1))
     def _():
         whole(c - 1, True)
 
-    def nearest_down():
-        @pl.when(has_down(c + 1))
-        def _():
-            @pl.when(jnp.logical_not(passes_down))
-            def _():
-                for hh in range(NH):
-                    each_piece(lambda p: z_copy(c + 1, hh, p, False).wait_recv())
-
-            whole(c + 1, True)
-
-    for d in range(2, C):
-        for hh in range(NH):
-
-            @pl.when(has_up(c - d))
-            def _():
-                streamed(c - d, hh, True)
-
-            if d == 2 and hh == 0:
-                nearest_down()
-
-            @pl.when(has_down(c + d))
-            def _():
-                streamed(c + d, hh, False)
-
-    if C == 2:
-        nearest_down()
+    ahead(1)
+
+    @pl.when(has_down(c + 1))
+    def _():
+        @pl.when(jnp.logical_not(passes_down))
+        def _():
+            for hh in range(NH):
+                each_piece(lambda p: z_copy(c + 1, hh, p, False).wait_recv())
+
+        whole(c + 1, True)
+
+    ahead(2)
+
+    @pl.when(has_up(c - 1))
+    def _():
+        settle_whole(c - 1, True)
+
+    ahead(3)
+    settle_whole(c, False)
+
+    @pl.when(has_down(c + 1))
+    def _():
+        settle_whole(c + 1, True)
+
+    steps = [(d, hh, up) for d in range(2, C) for hh in range(NH) for up in (True, False)]
+
+    def at_step(d, up, act):
+        src = c - d if up else c + d
+
+        @pl.when(has_up(src) if up else has_down(src))
+        def _():
+            act(src)
+
+    for n, (d, hh, up) in enumerate(steps):
+        early = 4 if d == 2 and hh == 0 and up else 0
+        at_step(d, up, lambda src: streamed(src, hh, up, early))
+        if n >= 2:
+            d0, hh0, up0 = steps[n - 2]
+            at_step(d0, up0, lambda src: settle(src, hh0, True))
+    for d0, hh0, up0 in steps[-2:]:
+        at_step(d0, up0, lambda src: settle(src, hh0, True))
 
     for t in range(NT):
         tile = a * NT + t
@@ -299,47 +385,26 @@
         @pl.when(here)
         def _():
             for hh in range(NH):
-
-                def arrived(other, _):
-                    source = (a + other) % A
-                    index = (t * A + source) * NH + hh
-                    pltpu.make_async_remote_copy(
-                        src_ref=recv_sum.at[t, source, hh],
-                        dst_ref=recv_sum.at[t, source, hh],
-                        send_sem=sum_send.at[0],
-                        recv_sem=sum_recv.at[index],
-                        device_id={"row": r, "col": c, "aux": source},
-                        device_id_type=MESH,
-                    ).wait_recv()
-                    kept[t, hh] = kept[t, hh] + recv_sum[t, source, hh].astype(jnp.float32)
-                    return 0
-
-                lax.fori_loop(1, A, arrived, 0)
                 for r2 in range(R):
                     out_ref[
                         t * T + hh * LANES : t * T + (hh + 1) * LANES, r2 * T : (r2 + 1) * T
-                    ] = kept[t, hh, r2].T
+                    ] = kept[tile, hh, r2].T
 
         @pl.when(jnp.logical_not(here))
         def _():
             for hh in range(NH):
                 for r2 in range(R):
-
-                    def add(source, total):
-                        index = ((t * A + source) * R + r2) * NH + hh
-                        pltpu.make_async_remote_copy(
-                            src_ref=recv_turn.at[t, source, r2, hh],
-                            dst_ref=recv_turn.at[t, source, r2, hh],
-                            send_sem=turn_send.at[0],
-                            recv_sem=turn_recv.at[index],
-                            device_id={"row": r2, "col": tile, "aux": source},
-                            device_id_type=MESH,
-                        ).wait_recv()
-                        return total + recv_turn[t, source, r2, hh].astype(jnp.float32)
-
+                    pltpu.make_async_remote_copy(
+                        src_ref=recv_turn.at[t, r2, hh],
+                        dst_ref=recv_turn.at[t, r2, hh],
+                        send_sem=turn_send.at[0],
+                        recv_sem=turn_recv.at[(t * R + r2) * NH + hh],
+                        device_id={"row": r2, "col": (c + 1) % C, "aux": a},
+                        device_id_type=MESH,
+                    ).wait_recv()
                     out_ref[
                         t * T : (t + 1) * T, r2 * T + hh * LANES : r2 * T + (hh + 1) * LANES
-                    ] = lax.fori_loop(0, A, add, jnp.zeros((T, LANES), jnp.float32))
+                    ] = recv_turn[t, r2, hh].astype(jnp.float32)
 
     for j in range(1, pairs):
         row_copy(r, peers[j], j).wait_send()
@@ -356,17 +421,24 @@
             each_piece(lambda p: z_copy(c, hh, p, False).wait_send())
 
     def finish(src, hh, up, turned):
+        def every_row(act):
+            lax.fori_loop(0, R, lambda r2, _: (act(r2), 0)[1], 0)
+
         if turned:
 
             @pl.when((c + 1 < C) if up else (c - 1 >= half_c))
             def _():
                 each_piece(lambda p: z_copy(src, hh, p, up).wait_send())
 
-            lax.fori_loop(0, R, lambda r2, _: (turn_copy(src, hh, r2).wait_send(), 0)[1], 0)
-
-        @pl.when(src // NT != a)
-        def _():
-            sum_copy(src, hh).wait_send()
+            @pl.when(c // NT == a)
+            def _():
+                every_row(lambda r2: turn_copy(src, hh, r2).wait_send())
+
+        each_other(
+            src,
+            turned,
+            lambda other: every_row(lambda r2: sum_copy(src, hh, r2, other).wait_send()),
+        )
 
     for hh in range(NH):
         finish(c, hh, True, False)
@@ -389,7 +461,7 @@
     occ = orbitals.shape[0]
     T = mb * blk
     kdim = occ * (width // blk)
-    NH, NT, pieces = T // LANES, C // A, 4
+    NH, NT, pieces = T // LANES, C // A, 6
     dims = (R, C, A, mb, occ, blk, cap, kdim, pieces)
     dma = pltpu.SemaphoreType.DMA
     bf16, f32 = jnp.bfloat16, jnp.float32
@@ -407,34 +479,37 @@
     result = pl.pallas_call(
         functools.partial(kernel, dims),
         out_shape=jax.ShapeDtypeStruct((NT * T, R * T), f32),
-        in_specs=[vmem] * 2,
+        in_specs=[pl.BlockSpec(memory_space=pl.ANY), vmem],
         out_specs=vmem,
         scratch_shapes=[
+            pltpu.VMEM((cap * blk, width), bf16),
             pltpu.VMEM((C, NH, kdim, LANES), bf16),
             pltpu.VMEM((R, T, kdim), bf16),
-            pltpu.VMEM((R, T, LANES), f32),
-            pltpu.VMEM((NT, NH, R, T, LANES), f32),
+            pltpu.VMEM((C, NH, R, T, LANES), f32),
             pltpu.VMEM((C, NH, R, T, LANES), bf16),
-            pltpu.VMEM((NT, A, NH, R, T, LANES), bf16),
-            pltpu.VMEM((NT, A, R, NH, T, LANES), bf16),
+            pltpu.VMEM((C, A, NH, R, T, LANES), bf16),
+            pltpu.VMEM((C, NH, R, T, LANES), bf16),
+            pltpu.VMEM((NT, R, NH, T, LANES), bf16),
+            dma(()),
             dma((C * NH * pieces,)),
             dma((C * NH * pieces,)),
             dma((C * NH * pieces,)),
             dma((R,)),
             dma((R,)),
-            dma((C * NH,)),
-            dma((NT * A * NH,)),
+            dma((C * A * NH * R,)),
+            dma((C * A * NH * R,)),
             dma((C * NH * R,)),
-            dma((NT * A * R * NH,)),
+            dma((NT * R * NH,)),
         ],
         compiler_params=pltpu.CompilerParams(
-            collective_id=0, has_side_effects=True, vmem_limit_bytes=50 * 1024 * 1024
+            collective_id=0, has_side_effects=True, vmem_limit_bytes=60 * 1024 * 1024
         ),
         cost_estimate=pl.CostEstimate(
             flops=2 * C * T * R * T * kdim, bytes_accessed=8 * 1024 * 1024, transcendentals=0
         ),
     )(
-        integrals.reshape(cap * blk, width), weights
+        integrals.reshape(cap * blk, width),
+        weights,
     )
     return result.reshape(NT * T, R, T)
 

time: 120 us -> 139 us (1.16)
  Pallas kernels: 117 us -> 136 us
    pallas_call x1, Pallas kernels: 114 us -> 134 us  [local(): pl.pallas_call(functools.partial(kernel, dims), out_shape=jax.ShapeDtypeS...]
where the time goes in v3:
time: 139 us
  Pallas kernels  136 us (98%)
  local copies, waits for them, and re-layouts  3.16 us (2%)
    pallas_call x1, Pallas kernels, local(): pl.pallas_call(functools.partial(kernel, dims), out_shape=jax.ShapeDtypeS...  134 us
    reshape x1, local copies, waits for them, and re-layouts, local(): return result.reshape(NT * T, R, T)  3.16 us

profile of v3, /device:TPU:7, one launch (start us, length us, event | category | flops | bytes accessed | tf_op | source)
XLA Modules:
  0.0 139.2 jit_solution(7381698462287739134)
XLA Ops:
  0.0 2.1 %shard_map.46.weights = bf16[256,512]{1,0:T(8,128)(2,1)} custom-call(s32[4,64]{1,0:T(4,128)} %bitcast.3, s32[4,64]{1,0:T(4,128)} %bitcast.4, bf16[64,4096]{1,0:T(8,128)(2,1)} %orb_ref.1), custom_call_target="tpu_custom_call" | custom-call | tf_op jit(solution)/shard_map/pallas_call | solution.py:469
  2.1 134.0 %shard_map.47 = f32[512,1024]{1,0:T(8,128)} custom-call(bf16[512,3072]{1,0:T(8,128)(2,1)} %bitcast.5, bf16[256,512]{1,0:T(8,128)(2,1)} %shard_map.46.weights), custom_call_target="tpu_custom_call" | custom-call | flops 6442450944 | bytes 8388608 | tf_op jit(solution)/shard_map/pallas_call | solution.py:479
  136.1 3.2 %reshape.15 = f32[512,4,256]{2,1,0:T(4,128)} reshape(f32[512,1024]{1,0:T(8,128)} %shard_map.47) | data formatting | bytes 4194304 | tf_op jit(solution)/shard_map/reshape | solution.py:514

commit v4 on v2

--- a/solution.py
+++ b/solution.py
@@ -45,9 +45,10 @@
 
 def kernel(
     dims,
-    packed_ref,
+    packed_hbm,
     weights,
     out_ref,
+    packed_ref,
     panel,
     column,
     block,
@@ -55,6 +56,7 @@
     send,
     recv_sum,
     recv_turn,
+    load,
     z_recv,
     z_up,
     z_down,
@@ -75,6 +77,8 @@
     devices = R * C * A
     me = (r * C + c) * A + a
 
+    loading = pltpu.make_async_copy(packed_hbm, packed_ref, load)
+    loading.start()
     barrier = pltpu.get_barrier_semaphore()
 
     def greet(k, _):
@@ -110,10 +114,6 @@
             column[r, hh * LANES : (hh + 1) * LANES, pl.ds(at, 256)] = tile.T.astype(jnp.bfloat16)
         return 0
 
-    lax.fori_loop(0, KDIM // 256, transform, 0)
-
-    pl.semaphore_wait(barrier, devices - 1)
-
     def z_copy(src, hh, p, up):
         ref = panel.at[src, hh, pl.ds(pl.multiple_of(p * step, step), step), :]
         target = jnp.minimum(c + 1, C - 1) if up else jnp.maximum(c - 1, 0)
@@ -127,12 +127,13 @@
             device_id_type=MESH,
         )
 
-    def row_copy(tile, target, send_index):
+    def row_copy(tile, target, send_index, p):
+        ref = column.at[tile, :, pl.ds(pl.multiple_of(p * step, step), step)]
         return pltpu.make_async_remote_copy(
-            src_ref=column.at[tile],
-            dst_ref=column.at[tile],
-            send_sem=row_send.at[send_index],
-            recv_sem=row_recv.at[tile],
+            src_ref=ref,
+            dst_ref=ref,
+            send_sem=row_send.at[send_index * PIECES + p],
+            recv_sem=row_recv.at[tile * PIECES + p],
             device_id={"row": target, "col": c, "aux": a},
             device_id_type=MESH,
         )
@@ -147,18 +148,39 @@
     peers = [(r + 2 * j) % R for j in range(pairs)]
     far = [(sibling + 2 * j) % R for j in range(pairs)]
 
-    for j in range(1, pairs):
-        row_copy(r, peers[j], j).start()
-    row_copy(r, sibling, 0).start()
-    for hh in range(NH):
-
+    def send_own(hh, p):
         @pl.when(sends_up)
         def _():
-            each_piece(lambda p: z_copy(c, hh, p, True).start())
+            z_copy(c, hh, p, True).start()
 
         @pl.when(sends_down)
         def _():
-            each_piece(lambda p: z_copy(c, hh, p, False).start())
+            z_copy(c, hh, p, False).start()
+
+    edge = half_c - 1
+    loading.wait()
+    pl.semaphore_wait(barrier, devices - 1)
+
+    def make_piece(p, _):
+        lax.fori_loop(p * (step // 256), (p + 1) * (step // 256), transform, 0)
+        for j in range(1, pairs):
+            row_copy(r, peers[j], j, p).start()
+        send_own(0, p)
+
+        @pl.when(c == edge)
+        def _():
+            for hh in range(1, NH):
+                send_own(hh, p)
+
+        row_copy(r, sibling, 0, p).start()
+        return 0
+
+    lax.fori_loop(0, PIECES, make_piece, 0)
+
+    @pl.when(c != edge)
+    def _():
+        for hh in range(1, NH):
+            each_piece(lambda p: send_own(hh, p))
 
     def has_up(src):
         return (src >= 0) & (src < half_c)
@@ -174,21 +196,31 @@
             z_copy(src, hh, p, up).start()
 
     passes_down = c - 1 >= half_c
-    for hh in range(NH):
-
-        @pl.when(has_up(c - 1))
-        def _():
-            each_piece(lambda p: take(c - 1, hh, p, True))
-
-        @pl.when(has_down(c + 1) & passes_down)
-        def _():
+
+    @pl.when(has_up(c - 1))
+    def _():
+        def one(n, _):
+            by_piece = c - 1 == edge
+            hh = jnp.where(by_piece, n % NH, n // PIECES)
+            p = jnp.where(by_piece, n // NH, n % PIECES)
+            take(c - 1, hh, p, True)
+            return 0
+
+        lax.fori_loop(0, NH * PIECES, one, 0)
+
+    @pl.when(has_down(c + 1) & passes_down)
+    def _():
+        for hh in range(NH):
             each_piece(lambda p: take(c + 1, hh, p, False))
 
+    def pass_row(j, p):
+        row_copy(peers[j], sibling, j, p).wait_recv()
+        row_copy(peers[j], sibling, pairs + j, p).start()
+
     for j in range(1, pairs):
-        row_copy(peers[j], sibling, j).wait_recv()
-        row_copy(peers[j], sibling, pairs + j).start()
+        each_piece(lambda p: pass_row(j, p))
     for j in range(pairs):
-        row_copy(far[j], sibling, 0).wait_recv()
+        each_piece(lambda p: row_copy(far[j], sibling, 0, p).wait_recv())
 
     def sum_copy(src, hh):
         return pltpu.make_async_remote_copy(
@@ -236,9 +268,12 @@
         for hh in range(NH):
             pass_sum(src, hh)
 
-    def streamed(src, hh, up):
+    def streamed(src, hh, up, taken):
         def piece(p, _):
-            take(src, hh, p, up)
+            @pl.when(p >= taken)
+            def _():
+                take(src, hh, p, up)
+
             rows = pl.ds(pl.multiple_of(p * step, step), step)
             for r2 in range(R):
                 value = jnp.dot(
@@ -258,13 +293,24 @@
         lax.fori_loop(0, R, one, 0)
         pass_sum(src, hh)
 
+    def ahead(p):
+        if C > 2:
+
+            @pl.when(has_up(c - 2))
+            def _():
+                take(c - 2, 0, p, True)
+
     block[...] = jnp.zeros_like(block)
+    ahead(0)
     whole(c, False)
+    ahead(1)
 
     @pl.when(has_up(c - 1))
     def _():
         whole(c - 1, True)
 
+    ahead(2)
+
     def nearest_down():
         @pl.when(has_down(c + 1))
         def _():
@@ -280,14 +326,14 @@
 
             @pl.when(has_up(c - d))
             def _():
-                streamed(c - d, hh, True)
+                streamed(c - d, hh, True, 3 if d == 2 and hh == 0 else 0)
 
             if d == 2 and hh == 0:
                 nearest_down()
 
             @pl.when(has_down(c + d))
             def _():
-                streamed(c + d, hh, False)
+                streamed(c + d, hh, False, 0)
 
     if C == 2:
         nearest_down()
@@ -341,10 +387,13 @@
                         t * T : (t + 1) * T, r2 * T + hh * LANES : r2 * T + (hh + 1) * LANES
                     ] = lax.fori_loop(0, A, add, jnp.zeros((T, LANES), jnp.float32))
 
-    for j in range(1, pairs):
-        row_copy(r, peers[j], j).wait_send()
-        row_copy(peers[j], sibling, pairs + j).wait_send()
-    row_copy(r, sibling, 0).wait_send()
+    def row_sent(p):
+        for j in range(1, pairs):
+            row_copy(r, peers[j], j, p).wait_send()
+            row_copy(peers[j], sibling, pairs + j, p).wait_send()
+        row_copy(r, sibling, 0, p).wait_send()
+
+    each_piece(row_sent)
     for hh in range(NH):
 
         @pl.when(sends_up)
@@ -389,7 +438,7 @@
     occ = orbitals.shape[0]
     T = mb * blk
     kdim = occ * (width // blk)
-    NH, NT, pieces = T // LANES, C // A, 4
+    NH, NT, pieces = T // LANES, C // A, 6
     dims = (R, C, A, mb, occ, blk, cap, kdim, pieces)
     dma = pltpu.SemaphoreType.DMA
     bf16, f32 = jnp.bfloat16, jnp.float32
@@ -407,9 +456,10 @@
     result = pl.pallas_call(
         functools.partial(kernel, dims),
         out_shape=jax.ShapeDtypeStruct((NT * T, R * T), f32),
-        in_specs=[vmem] * 2,
+        in_specs=[pl.BlockSpec(memory_space=pl.ANY), vmem],
         out_specs=vmem,
         scratch_shapes=[
+            pltpu.VMEM((cap * blk, width), bf16),
             pltpu.VMEM((C, NH, kdim, LANES), bf16),
             pltpu.VMEM((R, T, kdim), bf16),
             pltpu.VMEM((R, T, LANES), f32),
@@ -417,11 +467,12 @@
             pltpu.VMEM((C, NH, R, T, LANES), bf16),
             pltpu.VMEM((NT, A, NH, R, T, LANES), bf16),
             pltpu.VMEM((NT, A, R, NH, T, LANES), bf16),
+            dma(()),
             dma((C * NH * pieces,)),
             dma((C * NH * pieces,)),
             dma((C * NH * pieces,)),
-            dma((R,)),
-            dma((R,)),
+            dma((R * pieces,)),
+            dma((R * pieces,)),
             dma((C * NH,)),
             dma((NT * A * NH,)),
             dma((C * NH * R,)),
@@ -434,7 +485,8 @@
             flops=2 * C * T * R * T * kdim, bytes_accessed=8 * 1024 * 1024, transcendentals=0
         ),
     )(
-        integrals.reshape(cap * blk, width), weights
+        integrals.reshape(cap * blk, width),
+        weights,
     )
     return result.reshape(NT * T, R, T)
 

time: 120 us -> 115 us (0.958)
  Pallas kernels: 117 us -> 111 us
    pallas_call x1, Pallas kernels: 114 us -> 109 us  [local(): pl.pallas_call(functools.partial(kernel, dims), out_shape=jax.ShapeDtypeS...]
where the time goes in v4:
time: 115 us; the launch traced here: 114 us
  Pallas kernels  111 us (97%)
  local copies, waits for them, and re-layouts  2.94 us (3%)
    pallas_call x1, Pallas kernels, local(): pl.pallas_call(functools.partial(kernel, dims), out_shape=jax.ShapeDtypeS...  109 us

profile of v4, /device:TPU:7, one launch (start us, length us, event | category | flops | bytes accessed | tf_op | source)
XLA Modules:
  0.0 114.3 jit_solution(16748355572642350618)
XLA Ops:
  0.0 2.1 %shard_map.46.weights = bf16[256,512]{1,0:T(8,128)(2,1)} custom-call(s32[4,64]{1,0:T(4,128)} %bitcast.3, s32[4,64]{1,0:T(4,128)} %bitcast.4, bf16[64,4096]{1,0:T(8,128)(2,1)} %orb_ref.1), custom_call_target="tpu_custom_call" | custom-call | tf_op jit(solution)/shard_map/pallas_call | solution.py:446
  2.1 0.0 copy-start
  2.1 0.9 copy-done
  3.1 109.2 %shard_map.47 = f32[512,1024]{1,0:T(8,128)S(1)} custom-call(bf16[512,3072]{1,0:T(8,128)(2,1)} %bitcast.5, bf16[256,512]{1,0:T(8,128)(2,1)S(1)} %copy-done), custom_call_target="tpu_custom_call" | custom-call | flops 6442450944 | bytes 8388608 | tf_op jit(solution)/shard_map/pallas_call | solution.py:456
  112.3 2.0 %reshape.15 = f32[512,4,256]{2,1,0:T(4,128)} reshape(f32[512,1024]{1,0:T(8,128)S(1)} %shard_map.47) | data formatting | bytes 4194304 | tf_op jit(solution)/shard_map/reshape | solution.py:491
Async XLA Ops:
  2.1 0.9 copy-start

commit v5 on v4

--- a/solution.py
+++ b/solution.py
@@ -41,6 +41,10 @@
             weights[b * OCC : (b + 1) * OCC, p * LANES : (p + 1) * LANES] = jnp.where(
                 low, lo * lo_w, hi * hi_w
             ).astype(jnp.bfloat16)
+
+
+def row_parts(T):
+    return [(0, T // 2), (T // 2, T // 4), (3 * T // 4, T // 4)]
 
 
 def kernel(
@@ -69,7 +73,8 @@
 ):
     R, C, A, MB, OCC, BLK, CAP, KDIM, PIECES = dims
     T = MB * BLK
-    NH = T // LANES
+    parts = row_parts(T)
+    NH = len(parts)
     NT = C // A
     half_c = C // 2
     step = KDIM // PIECES
@@ -102,24 +107,25 @@
         h = jnp.dot(
             weights[...], packed_ref[:, pl.ds(at, 256)], preferred_element_type=jnp.float32
         )
-        for hh in range(NH):
-            parts = []
+        for hh in range(T // LANES):
+            quarters = []
             for j in range(2):
                 b0 = h[2 * hh * OCC : (2 * hh + 1) * OCC, j * LANES : (j + 1) * LANES]
                 b1 = h[(2 * hh + 1) * OCC : (2 * hh + 2) * OCC, j * LANES : (j + 1) * LANES]
-                parts.append(jnp.where(low, b0, pltpu.roll(b1, BLK, 1)))
-                parts.append(jnp.where(low, pltpu.roll(b0, BLK, 1), b1))
-            tile = jnp.concatenate(parts, axis=0)
-            panel[c, hh, pl.ds(at, 256), :] = tile.astype(jnp.bfloat16)
+                quarters.append(jnp.where(low, b0, pltpu.roll(b1, BLK, 1)))
+                quarters.append(jnp.where(low, pltpu.roll(b0, BLK, 1), b1))
+            tile = jnp.concatenate(quarters, axis=0)
             column[r, hh * LANES : (hh + 1) * LANES, pl.ds(at, 256)] = tile.T.astype(jnp.bfloat16)
         return 0
 
-    def z_copy(src, hh, p, up):
-        ref = panel.at[src, hh, pl.ds(pl.multiple_of(p * step, step), step), :]
+    def z_copy(src, hh, p, up, own=False):
+        start, size = parts[hh]
+        lanes = pl.ds(pl.multiple_of(p * step, step), step)
+        ref = panel.at[src, pl.ds(start, size), lanes]
         target = jnp.minimum(c + 1, C - 1) if up else jnp.maximum(c - 1, 0)
         index = (src * NH + hh) * PIECES + p
         return pltpu.make_async_remote_copy(
-            src_ref=ref,
+            src_ref=column.at[r, pl.ds(start, size), lanes] if own else ref,
             dst_ref=ref,
             send_sem=(z_up if up else z_down).at[index],
             recv_sem=z_recv.at[index],
@@ -151,11 +157,11 @@
     def send_own(hh, p):
         @pl.when(sends_up)
         def _():
-            z_copy(c, hh, p, True).start()
+            z_copy(c, hh, p, True, True).start()
 
         @pl.when(sends_down)
         def _():
-            z_copy(c, hh, p, False).start()
+            z_copy(c, hh, p, False, True).start()
 
     edge = half_c - 1
     loading.wait()
@@ -197,16 +203,18 @@
 
     passes_down = c - 1 >= half_c
 
-    @pl.when(has_up(c - 1))
+    @pl.when(has_up(c - 1) & (c - 1 == edge))
     def _():
-        def one(n, _):
-            by_piece = c - 1 == edge
-            hh = jnp.where(by_piece, n % NH, n // PIECES)
-            p = jnp.where(by_piece, n // NH, n % PIECES)
-            take(c - 1, hh, p, True)
-            return 0
-
-        lax.fori_loop(0, NH * PIECES, one, 0)
+        def every_part(p):
+            for hh in range(NH):
+                take(c - 1, hh, p, True)
+
+        each_piece(every_part)
+
+    @pl.when(has_up(c - 1) & (c - 1 != edge))
+    def _():
+        for hh in range(NH):
+            each_piece(lambda p: take(c - 1, hh, p, True))
 
     @pl.when(has_down(c + 1) & passes_down)
     def _():
@@ -223,9 +231,10 @@
         each_piece(lambda p: row_copy(far[j], sibling, 0, p).wait_recv())
 
     def sum_copy(src, hh):
+        rows = pl.ds(*parts[hh])
         return pltpu.make_async_remote_copy(
-            src_ref=send.at[src, hh],
-            dst_ref=recv_sum.at[src % NT, a, hh],
+            src_ref=send.at[src, :, rows],
+            dst_ref=recv_sum.at[src % NT, a, :, rows],
             send_sem=sum_send.at[src * NH + hh],
             recv_sem=sum_recv.at[((src % NT) * A + a) * NH + hh],
             device_id={"row": r, "col": c, "aux": src // NT},
@@ -233,9 +242,10 @@
         )
 
     def turn_copy(src, hh, r2):
+        rows = pl.ds(*parts[hh])
         return pltpu.make_async_remote_copy(
-            src_ref=send.at[src, hh, r2],
-            dst_ref=recv_turn.at[c % NT, a, r, hh],
+            src_ref=send.at[src, r2, rows],
+            dst_ref=recv_turn.at[c % NT, a, r, rows],
             send_sem=turn_send.at[(src * NH + hh) * R + r2],
             recv_sem=turn_recv.at[(((c % NT) * A + a) * R + r) * NH + hh],
             device_id={"row": r2, "col": src, "aux": c // NT},
@@ -243,25 +253,30 @@
         )
 
     def settle(src, hh, r2, value, turned):
-        send[src, hh, r2] = value.astype(jnp.bfloat16)
+        rows = pl.ds(*parts[hh])
+        send[src, r2, rows] = value.astype(jnp.bfloat16)
         if turned:
             turn_copy(src, hh, r2).start()
 
         @pl.when(src // NT == a)
         def _():
-            kept[src % NT, hh, r2] = value
+            kept[src % NT, r2, rows] = value
 
     def pass_sum(src, hh):
         @pl.when(src // NT != a)
         def _():
             sum_copy(src, hh).start()
 
+    def across(left, right):
+        return lax.dot_general(
+            left, right, (((1,), (1,)), ((), ())), preferred_element_type=jnp.float32
+        )
+
     def whole(src, turned):
         def one(r2, _):
-            tile = jnp.concatenate([panel[src, hh] for hh in range(NH)], axis=1)
-            value = jnp.dot(column[r2], tile, preferred_element_type=jnp.float32)
-            for hh in range(NH):
-                settle(src, hh, r2, value[:, hh * LANES : (hh + 1) * LANES], turned)
+            value = across(panel[src] if turned else column[r], column[r2])
+            for hh, (start, size) in enumerate(parts):
+                settle(src, hh, r2, value[start : start + size], turned)
             return 0
 
         lax.fori_loop(0, R, one, 0)
@@ -269,25 +284,24 @@
             pass_sum(src, hh)
 
     def streamed(src, hh, up, taken):
+        start, size = parts[hh]
+
         def piece(p, _):
             @pl.when(p >= taken)
             def _():
                 take(src, hh, p, up)
 
-            rows = pl.ds(pl.multiple_of(p * step, step), step)
+            lanes = pl.ds(pl.multiple_of(p * step, step), step)
             for r2 in range(R):
-                value = jnp.dot(
-                    column[r2, :, rows],
-                    panel[src, hh, rows, :],
-                    preferred_element_type=jnp.float32,
-                )
-                block[r2] = jnp.where(p == 0, value, block[r2] + value)
+                value = across(column[r2, :, lanes], panel[src, pl.ds(start, size), lanes])
+                old = block[r2, :, :size]
+                block[r2, :, :size] = jnp.where(p == 0, value, old + value)
             return 0
 
         lax.fori_loop(0, PIECES, piece, 0)
 
         def one(r2, _):
-            settle(src, hh, r2, block[r2], True)
+            settle(src, hh, r2, block[r2].T[:size], True)
             return 0
 
         lax.fori_loop(0, R, one, 0)
@@ -345,47 +359,48 @@
         @pl.when(here)
         def _():
             for hh in range(NH):
+                rows = pl.ds(*parts[hh])
 
                 def arrived(other, _):
                     source = (a + other) % A
                     index = (t * A + source) * NH + hh
                     pltpu.make_async_remote_copy(
-                        src_ref=recv_sum.at[t, source, hh],
-                        dst_ref=recv_sum.at[t, source, hh],
+                        src_ref=recv_sum.at[t, source, :, rows],
+                        dst_ref=recv_sum.at[t, source, :, rows],
                         send_sem=sum_send.at[0],
                         recv_sem=sum_recv.at[index],
                         device_id={"row": r, "col": c, "aux": source},
                         device_id_type=MESH,
                     ).wait_recv()
-                    kept[t, hh] = kept[t, hh] + recv_sum[t, source, hh].astype(jnp.float32)
+                    kept[t, :, rows] = kept[t, :, rows] + recv_sum[t, source, :, rows].astype(
+                        jnp.float32
+                    )
                     return 0
 
                 lax.fori_loop(1, A, arrived, 0)
-                for r2 in range(R):
-                    out_ref[
-                        t * T + hh * LANES : t * T + (hh + 1) * LANES, r2 * T : (r2 + 1) * T
-                    ] = kept[t, hh, r2].T
+            for r2 in range(R):
+                out_ref[t * T : (t + 1) * T, r2 * T : (r2 + 1) * T] = kept[t, r2]
 
         @pl.when(jnp.logical_not(here))
         def _():
-            for hh in range(NH):
-                for r2 in range(R):
-
-                    def add(source, total):
+            for r2 in range(R):
+
+                def add(source, total):
+                    for hh in range(NH):
+                        rows = pl.ds(*parts[hh])
                         index = ((t * A + source) * R + r2) * NH + hh
                         pltpu.make_async_remote_copy(
-                            src_ref=recv_turn.at[t, source, r2, hh],
-                            dst_ref=recv_turn.at[t, source, r2, hh],
+                            src_ref=recv_turn.at[t, source, r2, rows],
+                            dst_ref=recv_turn.at[t, source, r2, rows],
                             send_sem=turn_send.at[0],
                             recv_sem=turn_recv.at[index],
                             device_id={"row": r2, "col": tile, "aux": source},
                             device_id_type=MESH,
                         ).wait_recv()
-                        return total + recv_turn[t, source, r2, hh].astype(jnp.float32)
-
-                    out_ref[
-                        t * T : (t + 1) * T, r2 * T + hh * LANES : r2 * T + (hh + 1) * LANES
-                    ] = lax.fori_loop(0, A, add, jnp.zeros((T, LANES), jnp.float32))
+                    return total + recv_turn[t, source, r2].astype(jnp.float32)
+
+                total = lax.fori_loop(0, A, add, jnp.zeros((T, T), jnp.float32))
+                out_ref[t * T : (t + 1) * T, r2 * T : (r2 + 1) * T] = total.T
 
     def row_sent(p):
         for j in range(1, pairs):
@@ -398,11 +413,11 @@
 
         @pl.when(sends_up)
         def _():
-            each_piece(lambda p: z_copy(c, hh, p, True).wait_send())
+            each_piece(lambda p: z_copy(c, hh, p, True, True).wait_send())
 
         @pl.when(sends_down)
         def _():
-            each_piece(lambda p: z_copy(c, hh, p, False).wait_send())
+            each_piece(lambda p: z_copy(c, hh, p, False, True).wait_send())
 
     def finish(src, hh, up, turned):
         if turned:
@@ -438,7 +453,7 @@
     occ = orbitals.shape[0]
     T = mb * blk
     kdim = occ * (width // blk)
-    NH, NT, pieces = T // LANES, C // A, 6
+    NH, NT, pieces = len(row_parts(T)), C // A, 6
     dims = (R, C, A, mb, occ, blk, cap, kdim, pieces)
     dma = pltpu.SemaphoreType.DMA
     bf16, f32 = jnp.bfloat16, jnp.float32
@@ -460,13 +475,13 @@
         out_specs=vmem,
         scratch_shapes=[
             pltpu.VMEM((cap * blk, width), bf16),
-            pltpu.VMEM((C, NH, kdim, LANES), bf16),
+            pltpu.VMEM((C, T, kdim), bf16),
             pltpu.VMEM((R, T, kdim), bf16),
             pltpu.VMEM((R, T, LANES), f32),
-            pltpu.VMEM((NT, NH, R, T, LANES), f32),
-            pltpu.VMEM((C, NH, R, T, LANES), bf16),
-            pltpu.VMEM((NT, A, NH, R, T, LANES), bf16),
-            pltpu.VMEM((NT, A, R, NH, T, LANES), bf16),
+            pltpu.VMEM((NT, R, T, T), f32),
+            pltpu.VMEM((C, R, T, T), bf16),
+            pltpu.VMEM((NT, A, R, T, T), bf16),
+            pltpu.VMEM((NT, A, R, T, T), bf16),
             dma(()),
             dma((C * NH * pieces,)),
             dma((C * NH * pieces,)),

time: 115 us -> 114 us (level)
  no operation moved by 1% of the time
where the time goes in v5:
time: 114 us
  Pallas kernels  111 us (97%)
  local copies, waits for them, and re-layouts  2.94 us (3%)
    pallas_call x1, Pallas kernels, local(): pl.pallas_call(functools.partial(kernel, dims), out_shape=jax.ShapeDtypeS...  109 us

profile of v5, /device:TPU:7, one launch (start us, length us, event | category | flops | bytes accessed | tf_op | source)
XLA Modules:
  0.0 113.6 jit_solution(18095624068407893605)
XLA Ops:
  0.0 2.1 %shard_map.46.weights = bf16[256,512]{1,0:T(8,128)(2,1)} custom-call(s32[4,64]{1,0:T(4,128)} %bitcast.3, s32[4,64]{1,0:T(4,128)} %bitcast.4, bf16[64,4096]{1,0:T(8,128)(2,1)} %orb_ref.1), custom_call_target="tpu_custom_call" | custom-call | tf_op jit(solution)/shard_map/pallas_call | solution.py:461
  2.1 0.0 copy-start
  2.1 0.9 copy-done
  3.1 108.5 %shard_map.47 = f32[512,1024]{1,0:T(8,128)S(1)} custom-call(bf16[512,3072]{1,0:T(8,128)(2,1)} %bitcast.5, bf16[256,512]{1,0:T(8,128)(2,1)S(1)} %copy-done), custom_call_target="tpu_custom_call" | custom-call | flops 6442450944 | bytes 8388608 | tf_op jit(solution)/shard_map/pallas_call | solution.py:471
  111.6 2.0 %reshape.15 = f32[512,4,256]{2,1,0:T(4,128)} reshape(f32[512,1024]{1,0:T(8,128)S(1)} %shard_map.47) | data formatting | bytes 4194304 | tf_op jit(solution)/shard_map/reshape | solution.py:506
Async XLA Ops:
  2.1 0.9 copy-start

commit v6 on v5

--- a/solution.py
+++ b/solution.py
@@ -49,10 +49,9 @@
 
 def kernel(
     dims,
-    packed_hbm,
+    packed_ref,
     weights,
     out_ref,
-    packed_ref,
     panel,
     column,
     block,
@@ -60,7 +59,6 @@
     send,
     recv_sum,
     recv_turn,
-    load,
     z_recv,
     z_up,
     z_down,
@@ -82,8 +80,6 @@
     devices = R * C * A
     me = (r * C + c) * A + a
 
-    loading = pltpu.make_async_copy(packed_hbm, packed_ref, load)
-    loading.start()
     barrier = pltpu.get_barrier_semaphore()
 
     def greet(k, _):
@@ -164,11 +160,15 @@
             z_copy(c, hh, p, False, True).start()
 
     edge = half_c - 1
-    loading.wait()
+    first = step // 256
+    lax.fori_loop(0, first, transform, 0)
     pl.semaphore_wait(barrier, devices - 1)
 
     def make_piece(p, _):
-        lax.fori_loop(p * (step // 256), (p + 1) * (step // 256), transform, 0)
+        @pl.when(p > 0)
+        def _():
+            lax.fori_loop(p * first, (p + 1) * first, transform, 0)
+
         for j in range(1, pairs):
             row_copy(r, peers[j], j, p).start()
         send_own(0, p)
@@ -471,10 +471,9 @@
     result = pl.pallas_call(
         functools.partial(kernel, dims),
         out_shape=jax.ShapeDtypeStruct((NT * T, R * T), f32),
-        in_specs=[pl.BlockSpec(memory_space=pl.ANY), vmem],
+        in_specs=[vmem] * 2,
         out_specs=vmem,
         scratch_shapes=[
-            pltpu.VMEM((cap * blk, width), bf16),
             pltpu.VMEM((C, T, kdim), bf16),
             pltpu.VMEM((R, T, kdim), bf16),
             pltpu.VMEM((R, T, LANES), f32),
@@ -482,7 +481,6 @@
             pltpu.VMEM((C, R, T, T), bf16),
             pltpu.VMEM((NT, A, R, T, T), bf16),
             pltpu.VMEM((NT, A, R, T, T), bf16),
-            dma(()),
             dma((C * NH * pieces,)),
             dma((C * NH * pieces,)),
             dma((C * NH * pieces,)),

time: 114 us -> 113 us (level)
  no operation moved by 1% of the time
where the time goes in v6:
time: 113 us
  Pallas kernels  110 us (97%)
  local copies, waits for them, and re-layouts  2.94 us (3%)
    pallas_call x1, Pallas kernels, local(): pl.pallas_call(functools.partial(kernel, dims), out_shape=jax.ShapeDtypeS...  108 us

profile of v6, /device:TPU:7, one launch (start us, length us, event | category | flops | bytes accessed | tf_op | source)
XLA Modules:
  0.0 113.1 jit_solution(8801195479897426031)
XLA Ops:
  0.0 2.1 %shard_map.46.weights = bf16[256,512]{1,0:T(8,128)(2,1)} custom-call(s32[4,64]{1,0:T(4,128)} %bitcast.3, s32[4,64]{1,0:T(4,128)} %bitcast.4, bf16[64,4096]{1,0:T(8,128)(2,1)} %orb_ref.1), custom_call_target="tpu_custom_call" | custom-call | tf_op jit(solution)/shard_map/pallas_call | solution.py:461
  2.1 0.0 copy-start
  2.1 0.9 copy-done
  3.1 108.0 %shard_map.47 = f32[512,1024]{1,0:T(8,128)S(1)} custom-call(bf16[512,3072]{1,0:T(8,128)(2,1)} %bitcast.5, bf16[256,512]{1,0:T(8,128)(2,1)S(1)} %copy-done), custom_call_target="tpu_custom_call" | custom-call | flops 6442450944 | bytes 8388608 | tf_op jit(solution)/shard_map/pallas_call | solution.py:471
  111.1 2.0 %reshape.15 = f32[512,4,256]{2,1,0:T(4,128)} reshape(f32[512,1024]{1,0:T(8,128)S(1)} %shard_map.47) | data formatting | bytes 4194304 | tf_op jit(solution)/shard_map/reshape | solution.py:504
Async XLA Ops:
  2.1 0.9 copy-start

commit v7 on v6

--- a/solution.py
+++ b/solution.py
@@ -203,11 +203,19 @@
 
     passes_down = c - 1 >= half_c
 
-    @pl.when(has_up(c - 1) & (c - 1 == edge))
+    def pass_row(p):
+        for j in range(1, pairs):
+            row_copy(peers[j], sibling, j, p).wait_recv()
+            row_copy(peers[j], sibling, pairs + j, p).start()
+
+    beside = has_up(c - 1) & (c - 1 == edge)
+
+    @pl.when(beside)
     def _():
         def every_part(p):
             for hh in range(NH):
                 take(c - 1, hh, p, True)
+            pass_row(p)
 
         each_piece(every_part)
 
@@ -221,12 +229,10 @@
         for hh in range(NH):
             each_piece(lambda p: take(c + 1, hh, p, False))
 
-    def pass_row(j, p):
-        row_copy(peers[j], sibling, j, p).wait_recv()
-        row_copy(peers[j], sibling, pairs + j, p).start()
-
-    for j in range(1, pairs):
-        each_piece(lambda p: pass_row(j, p))
+    @pl.when(jnp.logical_not(beside))
+    def _():
+        each_piece(pass_row)
+
     for j in range(pairs):
         each_piece(lambda p: row_copy(far[j], sibling, 0, p).wait_recv())
 
@@ -316,13 +322,14 @@
 
     block[...] = jnp.zeros_like(block)
     ahead(0)
-    whole(c, False)
-    ahead(1)
+    if C == 2:
+        whole(c, False)
 
     @pl.when(has_up(c - 1))
     def _():
         whole(c - 1, True)
 
+    ahead(1)
     ahead(2)
 
     def nearest_down():
@@ -344,6 +351,7 @@
 
             if d == 2 and hh == 0:
                 nearest_down()
+                whole(c, False)
 
             @pl.when(has_down(c + d))
             def _():

time: 113 us -> 109 us (0.965)
  Pallas kernels: 110 us -> 106 us
    pallas_call x1, Pallas kernels: 108 us -> 104 us  [local(): pl.pallas_call(functools.partial(kernel, dims), out_shape=jax.ShapeDtypeS...]
where the time goes in v7:
time: 109 us
  Pallas kernels  106 us (97%)
  local copies, waits for them, and re-layouts  2.94 us (3%)
    pallas_call x1, Pallas kernels, local(): pl.pallas_call(functools.partial(kernel, dims), out_shape=jax.ShapeDtypeS...  104 us

profile of v7, /device:TPU:7, one launch (start us, length us, event | category | flops | bytes accessed | tf_op | source)
XLA Modules:
  0.0 109.1 jit_solution(2692764509968487760)
XLA Ops:
  0.0 2.1 %shard_map.46.weights = bf16[256,512]{1,0:T(8,128)(2,1)} custom-call(s32[4,64]{1,0:T(4,128)} %bitcast.3, s32[4,64]{1,0:T(4,128)} %bitcast.4, bf16[64,4096]{1,0:T(8,128)(2,1)} %orb_ref.1), custom_call_target="tpu_custom_call" | custom-call | tf_op jit(solution)/shard_map/pallas_call | solution.py:469
  2.1 0.0 copy-start
  2.1 0.9 copy-done
  3.1 104.0 %shard_map.47 = f32[512,1024]{1,0:T(8,128)S(1)} custom-call(bf16[512,3072]{1,0:T(8,128)(2,1)} %bitcast.5, bf16[256,512]{1,0:T(8,128)(2,1)S(1)} %copy-done), custom_call_target="tpu_custom_call" | custom-call | flops 6442450944 | bytes 8388608 | tf_op jit(solution)/shard_map/pallas_call | solution.py:479
  107.1 2.0 %reshape.15 = f32[512,4,256]{2,1,0:T(4,128)} reshape(f32[512,1024]{1,0:T(8,128)S(1)} %shard_map.47) | data formatting | bytes 4194304 | tf_op jit(solution)/shard_map/reshape | solution.py:512
Async XLA Ops:
  2.1 0.9 copy-start
